TPU v7x, 256 devices: a whole 4x4x8 slice. The times are simulated.
256 devices in a mesh: role: 2 (over x_lo), seq: 128 (over z, x_hi, y, core).
Axes of the slice: x: 4 (x_hi: 2, x_lo: 2; x = x_hi * 2 + x_lo), y: 4, z: 8, core: 2. Of those that a mesh axis runs over, the one named last changes fastest.
Arguments:
- queries: bfloat16 [3072, 4096], P('seq', 'role'), may hold values from -200 to 200
- keys: bfloat16 [3072, 4096], P('seq', 'role'), may hold values from -200 to 200
- values: bfloat16 [3072, 4096], P('seq', 'role'), may hold values from -6 to 6
- q_gain: float32 [4096], P('role'), may hold values from 1.5 to 4
- k_gain: float32 [4096], P('role'), may hold values from 1.5 to 4
Outputs:
- attended: bfloat16 [3072, 4096], P('seq', 'role')
All inputs are finite; a program needn't handle non-finite values.
Results may differ from a plain program's by a relative error of at most 0.0049.
The roundings to bfloat16 on the way count: a program that leaves them out, or rounds other values in their place, can miss the bound.
Values may be sent and summed in bfloat16 or wider, within the bound.
A program may use at most 64 MiB of HBM per device.

v0:
```python
import jax
import jax.numpy as jnp
from jax import lax
from jax.sharding import PartitionSpec as P

HEADS = 32
HEAD_DIM = 128
GRID_H = 30
GRID_W = 52


def pair_angles(positions):
    half_dim = HEAD_DIM // 2
    row_pairs = HEAD_DIM // 6
    time_pairs = half_dim - 2 * row_pairs
    frame_ids = positions // (GRID_H * GRID_W)
    row_ids = positions // GRID_W % GRID_H
    column_ids = positions % GRID_W
    pair_ids = jnp.arange(half_dim, dtype=jnp.int32)
    pair_float = pair_ids.astype(jnp.float32)
    in_frames = pair_ids < time_pairs
    in_rows = (pair_ids >= time_pairs) & (pair_ids < time_pairs + row_pairs)
    local_ids = jnp.where(
        in_frames,
        pair_float,
        jnp.where(in_rows, pair_float - time_pairs, pair_float - time_pairs - row_pairs),
    )
    span_width = jnp.where(in_frames, jnp.float32(2 * time_pairs), jnp.float32(2 * row_pairs))
    frequency = jnp.exp(-jnp.log(jnp.float32(10000.0)) * 2.0 * local_ids / span_width)
    coordinate = jnp.where(
        in_frames[None, :],
        frame_ids[:, None],
        jnp.where(in_rows[None, :], row_ids[:, None], column_ids[:, None]),
    )
    return coordinate.astype(jnp.float32) * frequency[None, :]


def rotate(stacked, angles):
    half_dim = HEAD_DIM // 2
    cosine = jnp.cos(angles)[:, None, :]
    sine_part = jnp.sin(angles)[:, None, :]
    front_half = stacked[..., :half_dim]
    back_half = stacked[..., half_dim:]
    return jnp.concatenate(
        [front_half * cosine - back_half * sine_part, front_half * sine_part + back_half * cosine],
        axis=-1,
    )


def attend_block(query_block, key_rows, value_rows, slab_rows):
    slab_count = key_rows.shape[0] // slab_rows
    block_rows = query_block.shape[0]

    def absorb(slab_index, carry):
        running_top, running_sum, weighted = carry
        scores = lax.dot_general(
            query_block, key_rows, (((1,), (1,)), ((), ())), preferred_element_type=jnp.float32
        )
        scores = scores * HEAD_DIM ** (-0.5)
        new_top = jnp.maximum(running_top, jnp.max(scores, axis=1, keepdims=True))
        exponents = jnp.exp(scores - new_top)
        fading = jnp.exp(running_top - new_top)
        running_sum = running_sum * fading + jnp.sum(exponents, axis=1, keepdims=True)
        weighted = weighted * fading + jnp.dot(
            exponents.astype(jnp.bfloat16), value_rows, preferred_element_type=jnp.float32
        )
        return (new_top, running_sum, weighted)

    start = (
        jnp.full((block_rows, 1), -jnp.inf, jnp.float32),
        jnp.zeros((block_rows, 1), jnp.float32),
        jnp.zeros((block_rows, HEAD_DIM), jnp.float32),
    )
    running_top, running_sum, weighted = lax.fori_loop(0, slab_count, absorb, start)
    return (weighted / running_sum).astype(jnp.bfloat16)


def on_device(queries, keys, values, q_gain, k_gain):
    tok_count, feature_local = queries.shape
    heads_here = feature_local // HEAD_DIM
    seq_count = lax.axis_size("seq")
    query_split = seq_count // heads_here
    rows_piece = tok_count // query_split
    feature_count = HEADS * HEAD_DIM
    q_float = queries.astype(jnp.float32)
    k_float = keys.astype(jnp.float32)
    q_total, k_total = lax.psum(
        (jnp.sum(q_float * q_float, axis=1), jnp.sum(k_float * k_float, axis=1)), "role"
    )
    positions = lax.axis_index("seq") * tok_count + jnp.arange(tok_count, dtype=jnp.int32)
    angles = pair_angles(positions)

    def prepare(as_float, total_sq, gain_row):
        normed = as_float * lax.rsqrt(total_sq / feature_count + 1e-06)[:, None] * gain_row[None, :]
        return rotate(normed.reshape(tok_count, heads_here, HEAD_DIM), angles).astype(jnp.bfloat16)

    q_rot = prepare(q_float, q_total, q_gain)
    k_rot = prepare(k_float, k_total, k_gain)
    v_heads = values.reshape(tok_count, heads_here, HEAD_DIM)

    def copies(stacked):
        widened = jnp.broadcast_to(stacked[:, None], (tok_count, query_split, heads_here, HEAD_DIM))
        return widened.reshape(tok_count, query_split * heads_here, HEAD_DIM)

    split_up = q_rot.reshape(query_split, rows_piece, heads_here, HEAD_DIM).transpose(1, 0, 2, 3)
    q_mine = lax.all_to_all(
        split_up.reshape(rows_piece, query_split * heads_here, HEAD_DIM),
        "seq",
        split_axis=1,
        concat_axis=0,
        tiled=True,
    )
    k_every = lax.all_to_all(copies(k_rot), "seq", split_axis=1, concat_axis=0, tiled=True)
    v_every = lax.all_to_all(copies(v_heads), "seq", split_axis=1, concat_axis=0, tiled=True)
    key_rows = k_every[:, 0]
    value_rows = v_every[:, 0]
    query_rows = q_mine[:, 0]
    query_count = query_rows.shape[0]
    key_count = key_rows.shape[0]

    def one_block(query_block):
        return attend_block(query_block, key_rows, value_rows, key_count)

    outputs = lax.map(
        one_block, query_rows.reshape(query_count // query_count, query_count, HEAD_DIM)
    )
    outputs = outputs.reshape(seq_count, rows_piece, HEAD_DIM)
    returned = lax.all_to_all(outputs, "seq", split_axis=0, concat_axis=0, tiled=True)
    arranged = returned.reshape(query_split, heads_here, rows_piece, HEAD_DIM).transpose(0, 2, 1, 3)
    return arranged.reshape(tok_count, feature_local)


def solution(mesh):
    in_specs = (P("seq", "role"), P("seq", "role"), P("seq", "role"), P("role"), P("role"))
    out_specs = P("seq", "role")
    return jax.shard_map(
        on_device, mesh=mesh, in_specs=in_specs, out_specs=out_specs, check_vma=False
    )
```

profile of v0, /device:TPU:1, one launch (start us, length us, event | category | flops | bytes accessed | tf_op | source)
XLA Modules:
  0.0 129.4 jit_solution(16868814442979013046)
XLA Ops:
  0.0 0.0 copy-start
  0.1 1.0 fusion.14
  1.1 1.0 fusion.17
  2.1 4.3 %all-reduce = (f32[24]{0:T(128)S(1)}, f32[24]{0:T(128)S(1)}) all-reduce(f32[24]{0:T(128)S(1)} %fusion.14, f32[24]{0:T(128)S(1)} %fusion.17), channel_id=1, replica_groups=mesh['role'=2,'seq'=128] {'role'}, use_global_device_ids=true, to_apply=%region_1.0 | all-reduce | flops 48 | bytes 384 | tf_op jit(solution)/shard_map/psum | solution.py:87
  6.5 1.0 fusion.16
  7.5 1.0 fusion.19
  8.6 0.1 fusion.21
  8.7 0.2 subtract_convert_fusion
  8.9 0.1 maximum_bitcast_fusion
  9.0 0.7 copy.17
  9.7 17.0 %all-to-all-start = ((bf16[3,128,128]{2,0,1:T(4,128)(2,1)}), bf16[3,128,128]{2,0,1:T(4,128)(2,1)S(1)}, u32[]{:S(2)}, u32[]{:S(2)}) async-start(bf16[3,128,128]{2,0,1:T(4,128)(2,1)} %copy.17), calls=%async_computation | async-start | bytes 262144 | tf_op jit(solution)/shard_map/all_to_all | solution.py:106
  26.7 0.1 pad_maximum_fusion
  26.9 13.4 %all-to-all-done = bf16[3,128,128]{2,0,1:T(4,128)(2,1)S(1)} async-done(((bf16[3,128,128]{2,0,1:T(4,128)(2,1)}), bf16[3,128,128]{2,0,1:T(4,128)(2,1)S(1)}, u32[]{:S(2)}, u32[]{:S(2)}) %all-to-all-start) | async-done | bytes 98336 | tf_op jit(solution)/shard_map/all_to_all | solution.py:106
  40.3 1.0 broadcast_in_dim.92
  41.3 5.6 %all-to-all-start.1 = ((bf16[24,128,128]{2,0,1:T(8,128)(2,1)}), bf16[24,128,128]{2,0,1:T(8,128)(2,1)S(1)}, u32[]{:S(2)}, u32[]{:S(2)}) async-start(bf16[24,128,128]{2,0,1:T(8,128)(2,1)} %bitcast.6), calls=%async_computation.1 | async-start | bytes 1572864 | tf_op jit(solution)/shard_map/all_to_all | solution.py:113
  46.9 0.0 copy-done
  46.9 25.4 %all-to-all-done.1 = bf16[24,128,128]{2,0,1:T(8,128)(2,1)S(1)} async-done(((bf16[24,128,128]{2,0,1:T(8,128)(2,1)}), bf16[24,128,128]{2,0,1:T(8,128)(2,1)S(1)}, u32[]{:S(2)}, u32[]{:S(2)}) %all-to-all-start.1) | async-done | bytes 786464 | tf_op jit(solution)/shard_map/all_to_all | solution.py:113
  72.3 1.0 broadcast_in_dim.94
  73.3 6.7 %all-to-all-start.2 = ((bf16[24,128,128]{2,0,1:T(8,128)(2,1)}), bf16[24,128,128]{2,0,1:T(8,128)(2,1)S(1)}, u32[]{:S(2)}, u32[]{:S(2)}) async-start(bf16[24,128,128]{2,0,1:T(8,128)(2,1)} %bitcast.10), calls=%async_computation.2 | async-start | bytes 1572864 | tf_op jit(solution)/shard_map/all_to_all | solution.py:114
  80.1 0.1 squeeze.11
  80.1 0.9 fusion.26
  81.0 0.0 copy-start.1
  81.0 2.1 %copy-done.1 = f32[384,3072]{1,0:T(8,128)} copy-done((f32[384,3072]{1,0:T(8,128)}, f32[384,3072]{1,0:T(8,128)S(1)}, u32[]{:S(2)}) %copy-start.1) | copy-done | bytes 4718616
  83.1 0.8 fusion
  83.9 21.6 %all-to-all-done.2 = bf16[24,128,128]{2,0,1:T(8,128)(2,1)S(1)} async-done(((bf16[24,128,128]{2,0,1:T(8,128)(2,1)}), bf16[24,128,128]{2,0,1:T(8,128)(2,1)S(1)}, u32[]{:S(2)}, u32[]{:S(2)}) %all-to-all-start.2) | async-done | bytes 786464 | tf_op jit(solution)/shard_map/all_to_all | solution.py:114
  105.5 3.2 %fusion.11 = bf16[384,128]{1,0:T(8,128)(2,1)S(1)} fusion(bf16[3072,128]{1,0:T(8,128)(2,1)S(1)} %bitcast.45, f32[384,3072]{1,0:T(8,128)} %copy-done.1, f32[384]{0:T(512)S(1)} %get-tuple-element.60, f32[384]{0:T(512)S(1)} %get-tuple-element.59, f32[384]{0:T(512)S(1)} %get-tuple-element.58), kind=kOutput, calls=%fused_computation.8 | convolution fusion | flops 304496640 | bytes 5607936 | tf_op jit(solution)/shard_map/while/body/eval_jaxpr/while/body/eval_jaxpr/dot_general | solution.py:64
  108.7 0.1 reshape.269
  108.7 20.0 %all_to_all.50 = bf16[128,3,128]{2,1,0:T(4,128)(2,1)S(1)} all-to-all(bf16[128,3,128]{2,1,0:T(4,128)(2,1)S(1)} %reshape.269), channel_id=1, replica_groups=mesh['role'=2,'seq'=128] {'seq'}, dimensions={0} | all-to-all | bytes 196608 | tf_op jit(solution)/shard_map/all_to_all | solution.py:128
  128.8 0.7 copy.27
  (12 shorter events, 0.2 us)
Async XLA Ops:
  0.0 46.9 %copy-start = (bf16[24,2048]{1,0:T(8,128)(2,1)S(1)}, bf16[24,2048]{1,0:T(8,128)(2,1)}, u32[]{:S(2)}) copy-start(bf16[24,2048]{1,0:T(8,128)(2,1)} %param.7) | copy-start | bytes 294916
  9.7 30.6 %all-to-all-start = ((bf16[3,128,128]{2,0,1:T(4,128)(2,1)}), bf16[3,128,128]{2,0,1:T(4,128)(2,1)S(1)}, u32[]{:S(2)}, u32[]{:S(2)}) async-start(bf16[3,128,128]{2,0,1:T(4,128)(2,1)} %copy.17), calls=%async_computation | async-start | bytes 262144 | tf_op jit(solution)/shard_map/all_to_all | solution.py:106
  41.3 31.0 %all-to-all-start.1 = ((bf16[24,128,128]{2,0,1:T(8,128)(2,1)}), bf16[24,128,128]{2,0,1:T(8,128)(2,1)S(1)}, u32[]{:S(2)}, u32[]{:S(2)}) async-start(bf16[24,128,128]{2,0,1:T(8,128)(2,1)} %bitcast.6), calls=%async_computation.1 | async-start | bytes 1572864 | tf_op jit(solution)/shard_map/all_to_all | solution.py:113
  73.3 32.2 %all-to-all-start.2 = ((bf16[24,128,128]{2,0,1:T(8,128)(2,1)}), bf16[24,128,128]{2,0,1:T(8,128)(2,1)S(1)}, u32[]{:S(2)}, u32[]{:S(2)}) async-start(bf16[24,128,128]{2,0,1:T(8,128)(2,1)} %bitcast.10), calls=%async_computation.2 | async-start | bytes 1572864 | tf_op jit(solution)/shard_map/all_to_all | solution.py:114
  81.0 2.1 %copy-start.1 = (f32[384,3072]{1,0:T(8,128)}, f32[384,3072]{1,0:T(8,128)S(1)}, u32[]{:S(2)}) copy-start(f32[384,3072]{1,0:T(8,128)S(1)} %get-tuple-element.61) | copy-start | bytes 14155780
where the time goes:
time: 130 us; the launch traced here: 129 us
  waiting for transfers between devices  60.4 us (46%)
  starting transfers between devices  29.3 us (23%)
  blocking collectives  24.4 us (19%)
  local copies, waits for them, and re-layouts  5.76 us (4%)
  other arithmetic  5.39 us (4%)
  matrix products  4.05 us (3%)
    all_to_all x1, waiting for transfers between devices, on_device(): lax.all_to_all(copies(k_rot), 'seq', split_axis=1, concat_axis=0, tiled=T...  25.4 us
    all_to_all x1, waiting for transfers between devices, on_device(): lax.all_to_all(copies(v_heads), 'seq', split_axis=1, concat_axis=0, tiled...  21.6 us
    all_to_all x1, blocking collectives, on_device(): lax.all_to_all(outputs, 'seq', split_axis=0, concat_axis=0, tiled=True)  20 us
    all_to_all x1, starting transfers between devices, on_device(): lax.all_to_all(split_up.reshape(rows_piece, query_split * heads_here, HEA...  17 us
    all_to_all x1, waiting for transfers between devices, on_device(): lax.all_to_all(split_up.reshape(rows_piece, query_split * heads_here, HEA...  13.4 us
    all_to_all x1, starting transfers between devices, on_device(): lax.all_to_all(copies(v_heads), 'seq', split_axis=1, concat_axis=0, tiled...  6.75 us
    all_to_all x1, starting transfers between devices, on_device(): lax.all_to_all(copies(k_rot), 'seq', split_axis=1, concat_axis=0, tiled=T...  5.57 us
    psum x1, blocking collectives, on_device(): lax.psum((jnp.sum(q_float * q_float, axis=1), jnp.sum(k_float * k_float,...  4.35 us
  transfers between devices with their start and end apart: 3, of which 3 were waited for; matrix products, arithmetic and copies ran while one was open for 1% of the time, Pallas kernels for 0%

commit v1 on v0

v1 whole, which is shorter than its diff:
```python
import math

import jax
import jax.numpy as jnp
from jax import lax
from jax.experimental import pallas as pl
from jax.experimental.pallas import tpu as pltpu
from jax.sharding import PartitionSpec as P

HEADS = 32
HEAD_DIM = 128
GRID_H = 30
GRID_W = 52
CORES = 2
RING = 4
GROUP = CORES * RING
MESH = pl.DeviceIdType.MESH


def angle_tables(first, rows):
    half_dim = HEAD_DIM // 2
    row_pairs = HEAD_DIM // 6
    time_pairs = half_dim - 2 * row_pairs
    lane = lax.broadcasted_iota(jnp.int32, (rows, HEAD_DIM), 1)
    pair = jnp.where(lane < half_dim, lane, lane - half_dim).astype(jnp.float32)
    position = (first + lax.broadcasted_iota(jnp.int32, (rows, HEAD_DIM), 0)).astype(jnp.float32)
    grid_row = jnp.floor((position + 0.5) / GRID_W)
    column = position - GRID_W * grid_row
    frame = jnp.floor((grid_row + 0.5) / GRID_H)
    row = grid_row - GRID_H * frame
    in_frames = pair < time_pairs
    in_rows = jnp.logical_and(pair >= time_pairs, pair < time_pairs + row_pairs)
    local = jnp.where(in_frames, pair, jnp.where(in_rows, pair - time_pairs, pair - time_pairs - row_pairs))
    width = jnp.where(in_frames, jnp.float32(2 * time_pairs), jnp.float32(2 * row_pairs))
    frequency = jnp.exp(-jnp.float32(math.log(10000.0)) * 2.0 * local / width)
    coordinate = jnp.where(in_frames, frame, jnp.where(in_rows, row, column))
    angle = coordinate * frequency
    sine = jnp.sin(angle)
    return jnp.cos(angle), jnp.where(lane < half_dim, -sine, sine)


def kernel(
    q_hbm, k_hbm, v_hbm, q_gain, k_gain, out_hbm,
    q_in, k_in, sums, q_send, k_send, q_land, k_all, v_all, out_send,
    in_sem, sum_sem, a_send, a_recv, g_send, g_recv, o_send, o_recv,
):
    role = lax.axis_index("role")
    seq = lax.axis_index("seq")
    tokens = q_in.shape[0]
    heads = q_send.shape[0]
    keys = heads * tokens
    mine = seq // GROUP
    place = seq % GROUP
    y = place // CORES
    core = place % CORES

    def at_place(other_y, other_core):
        return (role, mine * GROUP + lax.rem(other_y, RING) * CORES + other_core)

    sibling = at_place(y, 1 - core)
    after = at_place(y + 1, core)
    before = at_place(y + RING - 1, core)
    partner = (1 - role, seq)

    def peer(index):
        return (role, index * GROUP + place)

    q_copy = pltpu.make_async_copy(q_hbm, q_in, in_sem.at[0])
    k_copy = pltpu.make_async_copy(k_hbm, k_in, in_sem.at[1])
    q_copy.start()
    k_copy.start()

    barrier = pltpu.get_barrier_semaphore()

    def greet(step, carry):
        pl.semaphore_signal(barrier, inc=1, device_id=peer(lax.rem(mine + step, heads)), device_id_type=MESH)
        return carry

    for other in (partner, sibling, after, before):
        pl.semaphore_signal(barrier, inc=1, device_id=other, device_id_type=MESH)
    lax.fori_loop(1, heads, greet, 0)
    pl.semaphore_wait(barrier, heads + 3)

    def columns(index):
        return pl.ds(pl.multiple_of(index * HEAD_DIM, HEAD_DIM), HEAD_DIM)

    v_own = pltpu.make_async_copy(v_hbm.at[:, columns(mine)], v_all.at[0, mine], a_recv.at[2])
    v_own.start()

    def send_v(step, carry):
        to = lax.rem(mine + step, heads)
        pltpu.make_async_remote_copy(
            src_ref=v_hbm.at[:, columns(to)], dst_ref=v_all.at[0, mine],
            send_sem=a_send.at[2], recv_sem=a_recv.at[2], device_id=peer(to), device_id_type=MESH,
        ).start()
        return carry

    lax.fori_loop(1, heads, send_v, 0)

    q_copy.wait()
    k_copy.wait()

    def square_sum(ref):
        total = jnp.zeros((tokens, HEAD_DIM), jnp.float32)
        for head in range(heads):
            x = ref[:, head * HEAD_DIM:(head + 1) * HEAD_DIM].astype(jnp.float32)
            total = total + x * x
        return jnp.sum(total, axis=1, keepdims=True)

    lane = lax.broadcasted_iota(jnp.int32, (tokens, HEAD_DIM), 1)
    sums[0] = jnp.where(lane < HEAD_DIM // 2, square_sum(q_in), square_sum(k_in))
    sum_copy = pltpu.make_async_remote_copy(
        src_ref=sums.at[0], dst_ref=sums.at[1], send_sem=sum_sem.at[0], recv_sem=sum_sem.at[1],
        device_id=partner, device_id_type=MESH,
    )
    sum_copy.start()
    cosine, sine = angle_tables(seq * tokens, tokens)
    sum_copy.wait()
    scale = lax.rsqrt((sums[0] + sums[1]) / (HEADS * HEAD_DIM) + 1e-06)

    def prepare(source, factor, gain, target):
        for head in range(heads):
            x = source[:, head * HEAD_DIM:(head + 1) * HEAD_DIM].astype(jnp.float32)
            x = x * factor * gain[head:head + 1, :]
            x = x * cosine + pltpu.roll(x, HEAD_DIM // 2, 1) * sine
            target[head] = x.astype(jnp.bfloat16)

    def send_all(source, target, which):
        own = pltpu.make_async_copy(source.at[mine], target.at[mine], a_recv.at[which])
        own.start()

        def send(step, carry):
            to = lax.rem(mine + step, heads)
            pltpu.make_async_remote_copy(
                src_ref=source.at[to], dst_ref=target.at[mine],
                send_sem=a_send.at[which], recv_sem=a_recv.at[which], device_id=peer(to), device_id_type=MESH,
            ).start()
            return carry

        lax.fori_loop(1, heads, send, 0)

    prepare(k_in, scale[:, HEAD_DIM // 2:HEAD_DIM // 2 + 1], k_gain, k_send)
    send_all(k_send, k_all.at[0], 1)
    prepare(q_in, scale[:, 0:1], q_gain, q_send)
    send_all(q_send, q_land, 0)

    def wait_bytes(ref, sem):
        pltpu.make_async_copy(ref, ref, sem).wait()

    started = []

    def pass_on(array, kind, source, target, device):
        copy = pltpu.make_async_remote_copy(
            src_ref=array.at[source], dst_ref=array.at[target],
            send_sem=g_send.at[kind, target], recv_sem=g_recv.at[kind, target], device_id=device, device_id_type=MESH,
        )
        copy.start()
        started.append(copy)

    def arrived(array, kind, block):
        wait_bytes(array.at[block], g_recv.at[kind, block])

    for array, kind, which in ((v_all, 1, 2), (k_all, 0, 1)):
        wait_bytes(array.at[0], a_recv.at[which])
        pass_on(array, kind, 0, 1, after)
        pass_on(array, kind, 0, 2, before)
        pass_on(array, kind, 0, 4, sibling)

    arrived(v_all, 1, 2)
    pass_on(v_all, 1, 2, 3, before)
    pass_on(v_all, 1, 2, 6, sibling)
    arrived(v_all, 1, 1)
    pass_on(v_all, 1, 1, 5, sibling)

    wait_bytes(q_land, a_recv.at[0])
    query = q_land[...].reshape(keys, HEAD_DIM)
    to_exponent = math.log2(math.e) * HEAD_DIM ** (-0.5)

    def absorb(state, block):
        scores = lax.dot_general(
            query, k_all[block].reshape(keys, HEAD_DIM), (((1,), (1,)), ((), ())), preferred_element_type=jnp.float32
        )
        top = jnp.max(scores, axis=1, keepdims=True)
        if state is not None:
            top = jnp.maximum(top, state[0])
        exponents = jnp.exp2((scores - top) * to_exponent)
        total = jnp.sum(exponents, axis=1, keepdims=True)
        mixed = jnp.dot(
            exponents.astype(jnp.bfloat16), v_all[block].reshape(keys, HEAD_DIM), preferred_element_type=jnp.float32
        )
        if state is not None:
            fading = jnp.exp2((state[0] - top) * to_exponent)
            total = state[1] * fading + total
            mixed = state[2] * fading + mixed
        return top, total, mixed

    state = absorb(None, 0)
    arrived(k_all, 0, 1)
    pass_on(k_all, 0, 1, 3, after)
    pass_on(k_all, 0, 1, 5, sibling)
    arrived(v_all, 1, 4)
    arrived(k_all, 0, 4)
    state = absorb(state, 4)
    state = absorb(state, 1)
    arrived(k_all, 0, 2)
    pass_on(k_all, 0, 2, 6, sibling)
    arrived(v_all, 1, 3)
    pass_on(v_all, 1, 3, 7, sibling)
    state = absorb(state, 2)
    arrived(v_all, 1, 5)
    arrived(k_all, 0, 5)
    state = absorb(state, 5)
    arrived(k_all, 0, 3)
    pass_on(k_all, 0, 3, 7, sibling)
    arrived(v_all, 1, 6)
    arrived(k_all, 0, 6)
    state = absorb(state, 6)
    state = absorb(state, 3)
    arrived(v_all, 1, 7)
    arrived(k_all, 0, 7)
    state = absorb(state, 7)

    out_send[...] = (state[2] / state[1]).astype(jnp.bfloat16).reshape(heads, tokens, HEAD_DIM)
    own_out = pltpu.make_async_copy(out_send.at[mine], out_hbm.at[:, columns(mine)], o_recv)
    own_out.start()

    def send_back(step, carry):
        to = lax.rem(mine + step, heads)
        pltpu.make_async_remote_copy(
            src_ref=out_send.at[to], dst_ref=out_hbm.at[:, columns(mine)],
            send_sem=o_send, recv_sem=o_recv, device_id=peer(to), device_id_type=MESH,
        ).start()
        return carry

    lax.fori_loop(1, heads, send_back, 0)

    for copy in started:
        copy.wait_send()
    rest = pl.ds(0, heads - 1)
    wait_bytes(q_land.at[rest], a_send.at[0])
    wait_bytes(q_land.at[rest], a_send.at[1])
    wait_bytes(q_land.at[rest], a_send.at[2])
    wait_bytes(q_land.at[rest], o_send)
    wait_bytes(out_hbm, o_recv)


def on_device(queries, keys, values, q_gain, k_gain):
    tokens, features = queries.shape
    heads = features // HEAD_DIM
    bf16 = jnp.bfloat16
    anywhere = pl.BlockSpec(memory_space=pl.ANY)
    vmem = pl.BlockSpec(memory_space=pltpu.VMEM)
    return pl.pallas_call(
        kernel,
        out_shape=jax.ShapeDtypeStruct((tokens, features), bf16),
        in_specs=[anywhere, anywhere, anywhere, vmem, vmem],
        out_specs=anywhere,
        scratch_shapes=[
            pltpu.VMEM((tokens, features), bf16),
            pltpu.VMEM((tokens, features), bf16),
            pltpu.VMEM((2, tokens, HEAD_DIM), jnp.float32),
            pltpu.VMEM((heads, tokens, HEAD_DIM), bf16),
            pltpu.VMEM((heads, tokens, HEAD_DIM), bf16),
            pltpu.VMEM((heads, tokens, HEAD_DIM), bf16),
            pltpu.VMEM((GROUP, heads, tokens, HEAD_DIM), bf16),
            pltpu.VMEM((GROUP, heads, tokens, HEAD_DIM), bf16),
            pltpu.VMEM((heads, tokens, HEAD_DIM), bf16),
            pltpu.SemaphoreType.DMA((2,)),
            pltpu.SemaphoreType.DMA((2,)),
            pltpu.SemaphoreType.DMA((3,)),
            pltpu.SemaphoreType.DMA((3,)),
            pltpu.SemaphoreType.DMA((2, GROUP)),
            pltpu.SemaphoreType.DMA((2, GROUP)),
            pltpu.SemaphoreType.DMA,
            pltpu.SemaphoreType.DMA,
        ],
        compiler_params=pltpu.CompilerParams(
            collective_id=0, has_side_effects=True, vmem_limit_bytes=48 * 1024 * 1024
        ),
    )(queries, keys, values, q_gain.reshape(heads, HEAD_DIM), k_gain.reshape(heads, HEAD_DIM))


def solution(mesh):
    in_specs = (P("seq", "role"), P("seq", "role"), P("seq", "role"), P("role"), P("role"))
    out_specs = P("seq", "role")
    return jax.shard_map(
        on_device, mesh=mesh, in_specs=in_specs, out_specs=out_specs, check_vma=False
    )
```

time: 130 us -> 43.7 us (0.34)
  waiting for transfers between devices: 60.4 us -> 0 us
  Pallas kernels: 0 us -> 38.8 us
  starting transfers between devices: 29.3 us -> 0 us
  blocking collectives: 24.4 us -> 0 us
  other arithmetic: 5.39 us -> 0 us
  matrix products: 4.05 us -> 0 us
    all_to_all x3 -> x0, waiting for transfers between devices: 60.4 us -> none  [the longest x1 25.4 us: on_device(): lax.all_to_all(copies(k_rot), 'seq', split_axis=1, concat_axis=0, tiled=T...]
    pallas_call x0 -> x1, Pallas kernels: none -> 38.8 us  [on_device(): pl.pallas_call(kernel, out_shape=jax.ShapeDtypeStruct((tokens, features),...]
    all_to_all x3 -> x0, starting transfers between devices: 29.3 us -> none  [the longest x1 17 us: on_device(): lax.all_to_all(split_up.reshape(rows_piece, query_split * heads_here, HEA...]
    all_to_all x1 -> x0, blocking collectives: 20 us -> none  [on_device(): lax.all_to_all(outputs, 'seq', split_axis=0, concat_axis=0, tiled=True)]
    psum x1 -> x0, blocking collectives: 4.35 us -> none  [on_device(): lax.psum((jnp.sum(q_float * q_float, axis=1), jnp.sum(k_float * k_float,...]
    dot_general x2 -> x0, matrix products: 4.05 us -> none  [the longest x1 3.19 us: absorb(): jnp.dot(exponents.astype(jnp.bfloat16), value_rows, preferred_element_typ...]
    reduce_sum x3 -> x0, other arithmetic: 2.82 us -> none  [the longest x1 1.03 us: on_device(): jnp.sum(k_float * k_float, axis=1)]
    broadcast_in_dim x3 -> x0, local copies, waits for them, and re-layouts: 1.99 us -> none  [copies(): jnp.broadcast_to(stacked[:, None], (tok_count, query_split, heads_here, H...]
  transfers between devices with their start and end apart: 3 -> 0, of which waited for: 3 -> 0; matrix products, arithmetic and copies ran while one was open for 1% -> 0% of each run, Pallas kernels for 0% -> 0%
where the time goes in v1:
time: 43.7 us; the launch traced here: 43.5 us
  Pallas kernels  38.8 us (89%)
  local copies, waits for them, and re-layouts  4.71 us (11%)
    pallas_call x1, Pallas kernels, on_device(): pl.pallas_call(kernel, out_shape=jax.ShapeDtypeStruct((tokens, features),...  38.8 us
    unnamed x11, local copies, waits for them, and re-layouts  4.71 us

profile of v1, /device:TPU:1, one launch (start us, length us, event | category | flops | bytes accessed | tf_op | source)
XLA Modules:
  0.0 43.5 jit_solution(6300470024374150203)
XLA Ops:
  0.0 0.0 copy-start
  0.0 0.9 %copy-done = bf16[24,2048]{1,0:T(8,128)(2,1)S(1)} copy-done((bf16[24,2048]{1,0:T(8,128)(2,1)S(1)}, bf16[24,2048]{1,0:T(8,128)(2,1)}, u32[]{:S(2)}) %copy-start) | copy-done | bytes 98328
  0.9 0.0 copy-start.1
  0.9 0.9 %copy-done.1 = bf16[24,2048]{1,0:T(8,128)(2,1)S(1)} copy-done((bf16[24,2048]{1,0:T(8,128)(2,1)S(1)}, bf16[24,2048]{1,0:T(8,128)(2,1)}, u32[]{:S(2)}) %copy-start.1) | copy-done | bytes 98328
  1.8 0.0 copy-start.2
  1.8 0.9 %copy-done.2 = bf16[24,2048]{1,0:T(8,128)(2,1)S(1)} copy-done((bf16[24,2048]{1,0:T(8,128)(2,1)S(1)}, bf16[24,2048]{1,0:T(8,128)(2,1)}, u32[]{:S(2)}) %copy-start.2) | copy-done | bytes 98328
  2.7 0.0 copy-start.3
  2.7 0.7 %copy-done.3 = f32[2048]{0:T(1024)S(1)} copy-done((f32[2048]{0:T(1024)S(1)}, f32[2048]{0:T(1024)}, u32[]{:S(2)}) %copy-start.3) | copy-done | bytes 8216
  3.4 0.0 copy-start.4
  3.4 0.7 %copy-done.4 = f32[2048]{0:T(1024)S(1)} copy-done((f32[2048]{0:T(1024)S(1)}, f32[2048]{0:T(1024)}, u32[]{:S(2)}) %copy-start.4) | copy-done | bytes 8216
  4.1 38.8 %shard_map.55 = bf16[24,2048]{1,0:T(8,128)(2,1)S(1)} custom-call(bf16[24,2048]{1,0:T(8,128)(2,1)S(1)} %copy-done, bf16[24,2048]{1,0:T(8,128)(2,1)S(1)} %copy-done.1, bf16[24,2048]{1,0:T(8,128)(2,1)S(1)} %copy-done.2, f32[16,128]{1,0:T(8,128)S(1)} %bitcast.2, f32[16,128]{1,0:T(8,128)S(1)} %bitcast.3), custom_call_target="tpu_custom_call" | custom-call | tf_op jit(solution)/shard_map/pallas_call | solution.py:253
  42.8 0.6 %copy.7 = bf16[24,2048]{1,0:T(8,128)(2,1)} copy(bf16[24,2048]{1,0:T(8,128)(2,1)S(1)} %shard_map.55) | data formatting | bytes 196608
Async XLA Ops:
  0.0 0.9 %copy-start = (bf16[24,2048]{1,0:T(8,128)(2,1)S(1)}, bf16[24,2048]{1,0:T(8,128)(2,1)}, u32[]{:S(2)}) copy-start(bf16[24,2048]{1,0:T(8,128)(2,1)} %q_hbm.1) | copy-start | bytes 294916
  0.9 0.9 %copy-start.1 = (bf16[24,2048]{1,0:T(8,128)(2,1)S(1)}, bf16[24,2048]{1,0:T(8,128)(2,1)}, u32[]{:S(2)}) copy-start(bf16[24,2048]{1,0:T(8,128)(2,1)} %k_hbm.1) | copy-start | bytes 294916
  1.8 0.9 %copy-start.2 = (bf16[24,2048]{1,0:T(8,128)(2,1)S(1)}, bf16[24,2048]{1,0:T(8,128)(2,1)}, u32[]{:S(2)}) copy-start(bf16[24,2048]{1,0:T(8,128)(2,1)} %v_hbm.1) | copy-start | bytes 294916
  2.7 0.7 %copy-start.3 = (f32[2048]{0:T(1024)S(1)}, f32[2048]{0:T(1024)}, u32[]{:S(2)}) copy-start(f32[2048]{0:T(1024)} %param.8) | copy-start | bytes 24580
  3.4 0.7 %copy-start.4 = (f32[2048]{0:T(1024)S(1)}, f32[2048]{0:T(1024)}, u32[]{:S(2)}) copy-start(f32[2048]{0:T(1024)} %param.9) | copy-start | bytes 24580

commit v2 on v1

v2 whole, which is shorter than its diff:
```python
import math

import jax
import jax.numpy as jnp
from jax import lax
from jax.experimental import pallas as pl
from jax.experimental.pallas import tpu as pltpu
from jax.sharding import PartitionSpec as P

HEADS = 32
HEAD_DIM = 128
GRID_H = 30
GRID_W = 52
DEPTH = 8
CORES = 2
RING = 4
PLACES = CORES * RING
BATCH = 4
OFFSETS = (
    (0, 0), (1, 0), (7, 0), (0, 1),
    (2, 0), (6, 0), (1, 1), (7, 1),
    (3, 0), (5, 0), (2, 1), (6, 1),
    (4, 0), (3, 1), (5, 1), (4, 1),
)
MESH = pl.DeviceIdType.MESH


def angle_tables(first, rows):
    half_dim = HEAD_DIM // 2
    row_pairs = HEAD_DIM // 6
    time_pairs = half_dim - 2 * row_pairs
    lane = lax.broadcasted_iota(jnp.int32, (rows, HEAD_DIM), 1)
    pair = jnp.where(lane < half_dim, lane, lane - half_dim).astype(jnp.float32)
    position = (first + lax.broadcasted_iota(jnp.int32, (rows, HEAD_DIM), 0)).astype(jnp.float32)
    grid_row = jnp.floor((position + 0.5) / GRID_W)
    column = position - GRID_W * grid_row
    frame = jnp.floor((grid_row + 0.5) / GRID_H)
    row = grid_row - GRID_H * frame
    in_frames = pair < time_pairs
    in_rows = jnp.logical_and(pair >= time_pairs, pair < time_pairs + row_pairs)
    local = jnp.where(in_frames, pair, jnp.where(in_rows, pair - time_pairs, pair - time_pairs - row_pairs))
    width = jnp.where(in_frames, jnp.float32(2 * time_pairs), jnp.float32(2 * row_pairs))
    frequency = jnp.exp(-jnp.float32(math.log(10000.0)) * 2.0 * local / width)
    coordinate = jnp.where(in_frames, frame, jnp.where(in_rows, row, column))
    angle = coordinate * frequency
    sine = jnp.sin(angle)
    return jnp.cos(angle), jnp.where(lane < half_dim, -sine, sine)


def kernel(
    q_hbm, k_hbm, v_hbm, q_gain_hbm, k_gain_hbm, out_hbm,
    q_in, k_in, q_gain, k_gain, sums, q_send, k_send, q_land, k_all, v_all, out_send,
    in_sem, sum_sem, a_send, a_recv, y_send, y_recv, s_send, s_recv, o_send, o_recv,
):
    role = lax.axis_index("role")
    seq = lax.axis_index("seq")
    tokens = q_in.shape[0]
    heads = q_send.shape[0]
    keys = heads * tokens
    mine = seq // PLACES
    place = seq % PLACES
    z = mine // 2
    x = mine % 2
    y = place // CORES
    core = place % CORES

    loads = [
        pltpu.make_async_copy(source, target, in_sem.at[index])
        for index, (source, target) in enumerate(
            ((q_hbm, q_in), (k_hbm, k_in), (k_gain_hbm, k_gain), (q_gain_hbm, q_gain))
        )
    ]
    for load in loads:
        load.start()

    def home(index):
        dz, dx = OFFSETS[index]
        return lax.rem(z + dz, DEPTH) * 2 + (1 - x if dx else x)

    def server(index):
        dz, dx = OFFSETS[index]
        return lax.rem(z + DEPTH - dz, DEPTH) * 2 + (1 - x if dx else x)

    def peer(index):
        return (role, index * PLACES + place)

    def across(step):
        return (role, mine * PLACES + lax.rem(y + step, RING) * CORES + core)

    sibling = (role, mine * PLACES + y * CORES + 1 - core)
    partner = (1 - role, seq)
    far_first = range(heads - 1, 0, -1)

    barrier = pltpu.get_barrier_semaphore()
    for index in far_first:
        pl.semaphore_signal(barrier, inc=1, device_id=peer(server(index)), device_id_type=MESH)
    for other in (partner, sibling, across(1), across(2), across(3)):
        pl.semaphore_signal(barrier, inc=1, device_id=other, device_id_type=MESH)
    pl.semaphore_wait(barrier, heads + RING)

    def columns(index):
        return pl.ds(pl.multiple_of(index * HEAD_DIM, HEAD_DIM), HEAD_DIM)

    def remote(source, target, send_sem, recv_sem, device):
        pltpu.make_async_remote_copy(
            src_ref=source, dst_ref=target, send_sem=send_sem, recv_sem=recv_sem, device_id=device, device_id_type=MESH
        ).start()

    def wait_bytes(ref, sem):
        pltpu.make_async_copy(ref, ref, sem).wait()

    def exchange(pick, slot, kind):
        for index in far_first:
            to = server(index)
            remote(pick(to), slot(index), a_send.at[kind], a_recv.at[kind, index // BATCH], peer(to))
        pltpu.make_async_copy(pick(mine), slot(0), a_recv.at[kind, 0]).start()

    exchange(lambda to: v_hbm.at[:, columns(to)], lambda i: v_all.at[0, i // BATCH, 0, i % BATCH], 2)

    loads[0].wait()
    loads[1].wait()

    def square_sum(ref):
        total = jnp.zeros((tokens, HEAD_DIM), jnp.float32)
        for head in range(heads):
            rows = ref[:, head * HEAD_DIM:(head + 1) * HEAD_DIM].astype(jnp.float32)
            total = total + rows * rows
        return jnp.sum(total, axis=1, keepdims=True)

    lane = lax.broadcasted_iota(jnp.int32, (tokens, HEAD_DIM), 1)
    sums[0] = jnp.where(lane < HEAD_DIM // 2, square_sum(q_in), square_sum(k_in))
    sum_copy = pltpu.make_async_remote_copy(
        src_ref=sums.at[0], dst_ref=sums.at[1], send_sem=sum_sem.at[0], recv_sem=sum_sem.at[1],
        device_id=partner, device_id_type=MESH,
    )
    sum_copy.start()
    cosine, sine = angle_tables(seq * tokens, tokens)
    loads[2].wait()
    loads[3].wait()
    sum_copy.wait()
    scale = lax.rsqrt((sums[0] + sums[1]) / (HEADS * HEAD_DIM) + 1e-06)

    def prepare(source, factor, gain, target):
        for head in range(heads):
            rows = source[:, head * HEAD_DIM:(head + 1) * HEAD_DIM].astype(jnp.float32)
            rows = rows * factor * gain[head:head + 1, :]
            rows = rows * cosine + pltpu.roll(rows, HEAD_DIM // 2, 1) * sine
            target[head] = rows.astype(jnp.bfloat16)

    prepare(k_in, scale[:, HEAD_DIM // 2:HEAD_DIM // 2 + 1], k_gain, k_send)
    exchange(lambda to: k_send.at[to], lambda i: k_all.at[0, i // BATCH, 0, i % BATCH], 1)
    prepare(q_in, scale[:, 0:1], q_gain, q_send)
    exchange(lambda to: q_send.at[to], lambda i: q_land.at[i], 0)

    for array, kind in ((v_all, 2), (k_all, 1)):
        for batch in range(heads // BATCH):
            wait_bytes(array.at[0, batch, 0], a_recv.at[kind, batch])
            for step in (2, 1, 3):
                remote(
                    array.at[0, batch, 0], array.at[0, batch, step],
                    y_send.at[kind - 1], y_recv.at[kind - 1, batch], across(step),
                )

    def gathered(array, kind, batch):
        wait_bytes(array.at[0, batch, pl.ds(1, RING - 1)], y_recv.at[kind - 1, batch])
        remote(array.at[0, batch], array.at[1, batch], s_send.at[kind - 1], s_recv.at[kind - 1, batch], sibling)

    for batch in range(heads // BATCH):
        gathered(v_all, 2, batch)

    for batch in range(heads // BATCH):
        wait_bytes(q_land.at[pl.ds(batch * BATCH, BATCH)], a_recv.at[0, batch])
    query = q_land[...].reshape(keys, HEAD_DIM)
    to_exponent = math.log2(math.e) * HEAD_DIM ** (-0.5)

    def absorb(state, half, batch):
        if half:
            wait_bytes(v_all.at[1, batch], s_recv.at[1, batch])
            wait_bytes(k_all.at[1, batch], s_recv.at[0, batch])
        scores = lax.dot_general(
            query, k_all[half, batch].reshape(-1, HEAD_DIM), (((1,), (1,)), ((), ())),
            preferred_element_type=jnp.float32,
        )
        top = jnp.max(scores, axis=1, keepdims=True)
        if state is not None:
            top = jnp.maximum(top, state[0])
        exponents = jnp.exp2((scores - top) * to_exponent)
        total = jnp.sum(exponents, axis=1, keepdims=True)
        mixed = jnp.dot(
            exponents.astype(jnp.bfloat16), v_all[half, batch].reshape(-1, HEAD_DIM),
            preferred_element_type=jnp.float32,
        )
        if state is not None:
            fading = jnp.exp2((state[0] - top) * to_exponent)
            total = state[1] * fading + total
            mixed = state[2] * fading + mixed
        return top, total, mixed

    state = None
    for batch in range(heads // BATCH):
        gathered(k_all, 1, batch)
        if batch:
            state = absorb(state, 1, batch - 1)
        state = absorb(state, 0, batch)
    state = absorb(state, 1, heads // BATCH - 1)

    out_send[...] = (state[2] / state[1]).astype(jnp.bfloat16).reshape(heads, tokens, HEAD_DIM)
    for index in far_first:
        remote(out_send.at[index], out_hbm.at[:, columns(mine)], o_send, o_recv, peer(home(index)))
    pltpu.make_async_copy(out_send.at[0], out_hbm.at[:, columns(mine)], o_recv).start()

    for kind in range(3):
        wait_bytes(q_land.at[pl.ds(0, heads - 1)], a_send.at[kind])
    for array, kind in ((k_all, 0), (v_all, 1)):
        wait_bytes(array.at[0, pl.ds(0, RING - 1)], y_send.at[kind])
        wait_bytes(array.at[1], s_send.at[kind])
    wait_bytes(q_land.at[pl.ds(0, heads - 1)], o_send)
    wait_bytes(out_hbm, o_recv)


def on_device(queries, keys, values, q_gain, k_gain):
    tokens, features = queries.shape
    heads = features // HEAD_DIM
    batches = heads // BATCH
    bf16 = jnp.bfloat16
    in_hbm = pl.BlockSpec(memory_space=pltpu.HBM)
    return pl.pallas_call(
        kernel,
        out_shape=jax.ShapeDtypeStruct((tokens, features), bf16),
        in_specs=[in_hbm] * 5,
        out_specs=pl.BlockSpec(memory_space=pltpu.VMEM),
        scratch_shapes=[
            pltpu.VMEM((tokens, features), bf16),
            pltpu.VMEM((tokens, features), bf16),
            pltpu.VMEM((heads, HEAD_DIM), jnp.float32),
            pltpu.VMEM((heads, HEAD_DIM), jnp.float32),
            pltpu.VMEM((2, tokens, HEAD_DIM), jnp.float32),
            pltpu.VMEM((heads, tokens, HEAD_DIM), bf16),
            pltpu.VMEM((heads, tokens, HEAD_DIM), bf16),
            pltpu.VMEM((heads, tokens, HEAD_DIM), bf16),
            pltpu.VMEM((CORES, batches, RING, BATCH, tokens, HEAD_DIM), bf16),
            pltpu.VMEM((CORES, batches, RING, BATCH, tokens, HEAD_DIM), bf16),
            pltpu.VMEM((heads, tokens, HEAD_DIM), bf16),
            pltpu.SemaphoreType.DMA((4,)),
            pltpu.SemaphoreType.DMA((2,)),
            pltpu.SemaphoreType.DMA((3,)),
            pltpu.SemaphoreType.DMA((3, batches)),
            pltpu.SemaphoreType.DMA((2,)),
            pltpu.SemaphoreType.DMA((2, batches)),
            pltpu.SemaphoreType.DMA((2,)),
            pltpu.SemaphoreType.DMA((2, batches)),
            pltpu.SemaphoreType.DMA,
            pltpu.SemaphoreType.DMA,
        ],
        compiler_params=pltpu.CompilerParams(
            collective_id=0, has_side_effects=True, vmem_limit_bytes=40 * 1024 * 1024
        ),
    )(*(
        pltpu.with_memory_space_constraint(array, pltpu.HBM)
        for array in (queries, keys, values, q_gain.reshape(heads, HEAD_DIM), k_gain.reshape(heads, HEAD_DIM))
    ))


def solution(mesh):
    in_specs = (P("seq", "role"), P("seq", "role"), P("seq", "role"), P("role"), P("role"))
    out_specs = P("seq", "role")
    return jax.shard_map(
        on_device, mesh=mesh, in_specs=in_specs, out_specs=out_specs, check_vma=False
    )
```

time: 43.7 us -> 34.9 us (0.80)
  Pallas kernels: 38.8 us -> 34.2 us
  local copies, waits for them, and re-layouts: 4.71 us -> 0.64 us
    pallas_call x1, Pallas kernels: 38.8 us -> 34.2 us  [on_device(): pl.pallas_call(kernel, out_shape=jax.ShapeDtypeStruct((tokens, features),...]
    unnamed x11 -> x1, local copies, waits for them, and re-layouts: 4.71 us -> 0.64 us
where the time goes in v2:
time: 34.9 us; the launch traced here: 34.8 us
  Pallas kernels  34.2 us (98%)
  local copies, waits for them, and re-layouts  0.64 us (2%)
    pallas_call x1, Pallas kernels, on_device(): pl.pallas_call(kernel, out_shape=jax.ShapeDtypeStruct((tokens, features),...  34.2 us

profile of v2, /device:TPU:1, one launch (start us, length us, event | category | flops | bytes accessed | tf_op | source)
XLA Modules:
  0.0 34.8 jit_solution(58351238140286573)
XLA Ops:
  0.0 34.2 %shard_map.55 = bf16[24,2048]{1,0:T(8,128)(2,1)S(1)} custom-call(bf16[24,2048]{1,0:T(8,128)(2,1)} %q_hbm.1, bf16[24,2048]{1,0:T(8,128)(2,1)} %k_hbm.1, bf16[24,2048]{1,0:T(8,128)(2,1)} %v_hbm.1, f32[16,128]{1,0:T(8,128)} %bitcast.2, f32[16,128]{1,0:T(8,128)} %bitcast.3), custom_call_target="tpu_custom_call" | custom-call | tf_op jit(solution)/shard_map/pallas_call | solution.py:227
  34.2 0.6 %copy.7 = bf16[24,2048]{1,0:T(8,128)(2,1)} copy(bf16[24,2048]{1,0:T(8,128)(2,1)S(1)} %shard_map.55) | data formatting | bytes 196608

commit v3 on v2

--- a/solution.py
+++ b/solution.py
@@ -22,6 +22,8 @@
     (3, 0), (5, 0), (2, 1), (6, 1),
     (4, 0), (3, 1), (5, 1), (4, 1),
 )
+PIECE = 2
+RELAY = (None, (0, 0, 0, 0), (1, 2, 1, 2))
 MESH = pl.DeviceIdType.MESH
 
 
@@ -112,7 +114,7 @@
     def exchange(pick, slot, kind):
         for index in far_first:
             to = server(index)
-            remote(pick(to), slot(index), a_send.at[kind], a_recv.at[kind, index // BATCH], peer(to))
+            remote(pick(to), slot(index), a_send.at[kind], a_recv.at[kind, index // PIECE], peer(to))
         pltpu.make_async_copy(pick(mine), slot(0), a_recv.at[kind, 0]).start()
 
     exchange(lambda to: v_hbm.at[:, columns(to)], lambda i: v_all.at[0, i // BATCH, 0, i % BATCH], 2)
@@ -152,24 +154,42 @@
     prepare(q_in, scale[:, 0:1], q_gain, q_send)
     exchange(lambda to: q_send.at[to], lambda i: q_land.at[i], 0)
 
-    for array, kind in ((v_all, 2), (k_all, 1)):
-        for batch in range(heads // BATCH):
-            wait_bytes(array.at[0, batch, 0], a_recv.at[kind, batch])
-            for step in (2, 1, 3):
+    batches = heads // BATCH
+
+    def spread(array, kind, batch):
+        for piece in range(batch * BATCH // PIECE, (batch + 1) * BATCH // PIECE):
+            rows = pl.ds(piece * PIECE % BATCH, PIECE)
+            own = array.at[0, batch, 0, rows]
+            wait_bytes(own, a_recv.at[kind, piece])
+            for step, slot in ((2, 3), (1, 1), (3, 2)) if RELAY[kind][batch] == 0 else ((1, 1), (3, 2)):
                 remote(
-                    array.at[0, batch, 0], array.at[0, batch, step],
-                    y_send.at[kind - 1], y_recv.at[kind - 1, batch], across(step),
+                    own, array.at[0, batch, slot, rows],
+                    y_send.at[kind - 1], y_recv.at[kind - 1, batch, slot - 1], across(step),
                 )
 
+    def relay(array, kind, batch):
+        slot = RELAY[kind][batch]
+        if slot:
+            wait_bytes(array.at[0, batch, slot], y_recv.at[kind - 1, batch, slot - 1])
+            remote(
+                array.at[0, batch, slot], array.at[0, batch, 3],
+                y_send.at[kind - 1], y_recv.at[kind - 1, batch, 2], across(1 if slot == 1 else 3),
+            )
+
     def gathered(array, kind, batch):
-        wait_bytes(array.at[0, batch, pl.ds(1, RING - 1)], y_recv.at[kind - 1, batch])
+        for slot in (1, 2, 3):
+            if slot != RELAY[kind][batch]:
+                wait_bytes(array.at[0, batch, slot], y_recv.at[kind - 1, batch, slot - 1])
         remote(array.at[0, batch], array.at[1, batch], s_send.at[kind - 1], s_recv.at[kind - 1, batch], sibling)
 
-    for batch in range(heads // BATCH):
-        gathered(v_all, 2, batch)
-
-    for batch in range(heads // BATCH):
-        wait_bytes(q_land.at[pl.ds(batch * BATCH, BATCH)], a_recv.at[0, batch])
+    for batch in range(batches):
+        spread(v_all, 2, batch)
+    for batch in range(batches):
+        spread(k_all, 1, batch)
+        relay(v_all, 2, batch)
+
+    for piece in range(heads // PIECE):
+        wait_bytes(q_land.at[pl.ds(piece * PIECE, PIECE)], a_recv.at[0, piece])
     query = q_land[...].reshape(keys, HEAD_DIM)
     to_exponent = math.log2(math.e) * HEAD_DIM ** (-0.5)
 
@@ -197,12 +217,13 @@
         return top, total, mixed
 
     state = None
-    for batch in range(heads // BATCH):
-        gathered(k_all, 1, batch)
+    for batch in range(batches):
+        for array, kind in ((k_all, 1), (v_all, 2)):
+            gathered(array, kind, batch)
         if batch:
             state = absorb(state, 1, batch - 1)
         state = absorb(state, 0, batch)
-    state = absorb(state, 1, heads // BATCH - 1)
+    state = absorb(state, 1, batches - 1)
 
     out_send[...] = (state[2] / state[1]).astype(jnp.bfloat16).reshape(heads, tokens, HEAD_DIM)
     for index in far_first:
@@ -244,9 +265,9 @@
             pltpu.SemaphoreType.DMA((4,)),
             pltpu.SemaphoreType.DMA((2,)),
             pltpu.SemaphoreType.DMA((3,)),
-            pltpu.SemaphoreType.DMA((3, batches)),
+            pltpu.SemaphoreType.DMA((3, heads // PIECE)),
             pltpu.SemaphoreType.DMA((2,)),
-            pltpu.SemaphoreType.DMA((2, batches)),
+            pltpu.SemaphoreType.DMA((2, batches, RING - 1)),
             pltpu.SemaphoreType.DMA((2,)),
             pltpu.SemaphoreType.DMA((2, batches)),
             pltpu.SemaphoreType.DMA,

time: 34.9 us -> 33.9 us (0.971)
  Pallas kernels: 34.2 us -> 33.2 us
    pallas_call x1, Pallas kernels: 34.2 us -> 33.2 us  [on_device(): pl.pallas_call(kernel, out_shape=jax.ShapeDtypeStruct((tokens, features),...]
where the time goes in v3:
time: 33.9 us
  Pallas kernels  33.2 us (98%)
  local copies, waits for them, and re-layouts  0.64 us (2%)
    pallas_call x1, Pallas kernels, on_device(): pl.pallas_call(kernel, out_shape=jax.ShapeDtypeStruct((tokens, features),...  33.2 us

profile of v3, /device:TPU:1, one launch (start us, length us, event | category | flops | bytes accessed | tf_op | source)
XLA Modules:
  0.0 33.9 jit_solution(4713202270155059837)
XLA Ops:
  0.0 33.2 %shard_map.55 = bf16[24,2048]{1,0:T(8,128)(2,1)S(1)} custom-call(bf16[24,2048]{1,0:T(8,128)(2,1)} %q_hbm.1, bf16[24,2048]{1,0:T(8,128)(2,1)} %k_hbm.1, bf16[24,2048]{1,0:T(8,128)(2,1)} %v_hbm.1, f32[16,128]{1,0:T(8,128)} %bitcast.2, f32[16,128]{1,0:T(8,128)} %bitcast.3), custom_call_target="tpu_custom_call" | custom-call | tf_op jit(solution)/shard_map/pallas_call | solution.py:248
  33.2 0.6 %copy.7 = bf16[24,2048]{1,0:T(8,128)(2,1)} copy(bf16[24,2048]{1,0:T(8,128)(2,1)S(1)} %shard_map.55) | data formatting | bytes 196608

commit v4 on v3

--- a/solution.py
+++ b/solution.py
@@ -1,3 +1,4 @@
+import functools
 import math
 
 import jax
@@ -51,7 +52,7 @@
 
 def kernel(
     q_hbm, k_hbm, v_hbm, q_gain_hbm, k_gain_hbm, out_hbm,
-    q_in, k_in, q_gain, k_gain, sums, q_send, k_send, q_land, k_all, v_all, out_send,
+    q_in, k_in, v_in, q_gain, k_gain, sums, q_send, k_send, q_land, k_all, v_all, out_send,
     in_sem, sum_sem, a_send, a_recv, y_send, y_recv, s_send, s_recv, o_send, o_recv,
 ):
     role = lax.axis_index("role")
@@ -69,7 +70,7 @@
     loads = [
         pltpu.make_async_copy(source, target, in_sem.at[index])
         for index, (source, target) in enumerate(
-            ((q_hbm, q_in), (k_hbm, k_in), (k_gain_hbm, k_gain), (q_gain_hbm, q_gain))
+            ((q_hbm, q_in), (k_hbm, k_in), (k_gain_hbm, k_gain), (q_gain_hbm, q_gain), (v_hbm, v_in))
         )
     ]
     for load in loads:
@@ -92,33 +93,17 @@
     sibling = (role, mine * PLACES + y * CORES + 1 - core)
     partner = (1 - role, seq)
     far_first = range(heads - 1, 0, -1)
+    servers = [server(index) for index in range(heads)]
+    homes = [home(index) for index in range(heads)]
+    server_peers = [peer(index) for index in servers]
+    home_peers = [peer(index) for index in homes]
+    ring = [across(step) for step in range(RING)]
 
     barrier = pltpu.get_barrier_semaphore()
     for index in far_first:
-        pl.semaphore_signal(barrier, inc=1, device_id=peer(server(index)), device_id_type=MESH)
-    for other in (partner, sibling, across(1), across(2), across(3)):
+        pl.semaphore_signal(barrier, inc=1, device_id=server_peers[index], device_id_type=MESH)
+    for other in (partner, sibling, ring[1], ring[2], ring[3]):
         pl.semaphore_signal(barrier, inc=1, device_id=other, device_id_type=MESH)
-    pl.semaphore_wait(barrier, heads + RING)
-
-    def columns(index):
-        return pl.ds(pl.multiple_of(index * HEAD_DIM, HEAD_DIM), HEAD_DIM)
-
-    def remote(source, target, send_sem, recv_sem, device):
-        pltpu.make_async_remote_copy(
-            src_ref=source, dst_ref=target, send_sem=send_sem, recv_sem=recv_sem, device_id=device, device_id_type=MESH
-        ).start()
-
-    def wait_bytes(ref, sem):
-        pltpu.make_async_copy(ref, ref, sem).wait()
-
-    def exchange(pick, slot, kind):
-        for index in far_first:
-            to = server(index)
-            remote(pick(to), slot(index), a_send.at[kind], a_recv.at[kind, index // PIECE], peer(to))
-        pltpu.make_async_copy(pick(mine), slot(0), a_recv.at[kind, 0]).start()
-
-    exchange(lambda to: v_hbm.at[:, columns(to)], lambda i: v_all.at[0, i // BATCH, 0, i % BATCH], 2)
-
     loads[0].wait()
     loads[1].wait()
 
@@ -131,14 +116,38 @@
 
     lane = lax.broadcasted_iota(jnp.int32, (tokens, HEAD_DIM), 1)
     sums[0] = jnp.where(lane < HEAD_DIM // 2, square_sum(q_in), square_sum(k_in))
+    cosine, sine = angle_tables(seq * tokens, tokens)
+    loads[2].wait()
+    loads[3].wait()
+    loads[4].wait()
+    pl.semaphore_wait(barrier, heads + RING)
+
+    def columns(index):
+        return pl.ds(pl.multiple_of(index * HEAD_DIM, HEAD_DIM), HEAD_DIM)
+
+    def remote(source, target, send_sem, recv_sem, device):
+        pltpu.make_async_remote_copy(
+            src_ref=source, dst_ref=target, send_sem=send_sem, recv_sem=recv_sem, device_id=device, device_id_type=MESH
+        ).start()
+
+    def wait_bytes(ref, sem):
+        pltpu.make_async_copy(ref, ref, sem).wait()
+
+    def exchange(pick, slot, kind):
+        for index in far_first:
+            remote(
+                pick(servers[index]), slot(index), a_send.at[kind], a_recv.at[kind, index // PIECE],
+                server_peers[index],
+            )
+        pltpu.make_async_copy(pick(mine), slot(0), a_recv.at[kind, 0]).start()
+
+    exchange(lambda to: v_in.at[:, columns(to)], lambda i: v_all.at[0, i // BATCH, 0, i % BATCH], 2)
+
     sum_copy = pltpu.make_async_remote_copy(
         src_ref=sums.at[0], dst_ref=sums.at[1], send_sem=sum_sem.at[0], recv_sem=sum_sem.at[1],
         device_id=partner, device_id_type=MESH,
     )
     sum_copy.start()
-    cosine, sine = angle_tables(seq * tokens, tokens)
-    loads[2].wait()
-    loads[3].wait()
     sum_copy.wait()
     scale = lax.rsqrt((sums[0] + sums[1]) / (HEADS * HEAD_DIM) + 1e-06)
 
@@ -164,7 +173,7 @@
             for step, slot in ((2, 3), (1, 1), (3, 2)) if RELAY[kind][batch] == 0 else ((1, 1), (3, 2)):
                 remote(
                     own, array.at[0, batch, slot, rows],
-                    y_send.at[kind - 1], y_recv.at[kind - 1, batch, slot - 1], across(step),
+                    y_send.at[kind - 1], y_recv.at[kind - 1, batch, slot - 1], ring[step],
                 )
 
     def relay(array, kind, batch):
@@ -173,7 +182,7 @@
             wait_bytes(array.at[0, batch, slot], y_recv.at[kind - 1, batch, slot - 1])
             remote(
                 array.at[0, batch, slot], array.at[0, batch, 3],
-                y_send.at[kind - 1], y_recv.at[kind - 1, batch, 2], across(1 if slot == 1 else 3),
+                y_send.at[kind - 1], y_recv.at[kind - 1, batch, 2], ring[1 if slot == 1 else 3],
             )
 
     def gathered(array, kind, batch):
@@ -193,23 +202,30 @@
     query = q_land[...].reshape(keys, HEAD_DIM)
     to_exponent = math.log2(math.e) * HEAD_DIM ** (-0.5)
 
-    def absorb(state, half, batch):
-        if half:
-            wait_bytes(v_all.at[1, batch], s_recv.at[1, batch])
-            wait_bytes(k_all.at[1, batch], s_recv.at[0, batch])
-        scores = lax.dot_general(
-            query, k_all[half, batch].reshape(-1, HEAD_DIM), (((1,), (1,)), ((), ())),
-            preferred_element_type=jnp.float32,
-        )
-        top = jnp.max(scores, axis=1, keepdims=True)
+    def absorb(state, blocks):
+        for half, batch in blocks:
+            if half:
+                wait_bytes(v_all.at[1, batch], s_recv.at[1, batch])
+                wait_bytes(k_all.at[1, batch], s_recv.at[0, batch])
+        scores = [
+            lax.dot_general(
+                query, k_all[half, batch].reshape(-1, HEAD_DIM), (((1,), (1,)), ((), ())),
+                preferred_element_type=jnp.float32,
+            )
+            for half, batch in blocks
+        ]
+        top = jnp.max(functools.reduce(jnp.maximum, scores), axis=1, keepdims=True)
         if state is not None:
             top = jnp.maximum(top, state[0])
-        exponents = jnp.exp2((scores - top) * to_exponent)
-        total = jnp.sum(exponents, axis=1, keepdims=True)
-        mixed = jnp.dot(
-            exponents.astype(jnp.bfloat16), v_all[half, batch].reshape(-1, HEAD_DIM),
-            preferred_element_type=jnp.float32,
-        )
+        exponents = [jnp.exp2((block - top) * to_exponent) for block in scores]
+        total = jnp.sum(functools.reduce(jnp.add, exponents), axis=1, keepdims=True)
+        mixed = functools.reduce(jnp.add, [
+            jnp.dot(
+                weights.astype(jnp.bfloat16), v_all[half, batch].reshape(-1, HEAD_DIM),
+                preferred_element_type=jnp.float32,
+            )
+            for weights, (half, batch) in zip(exponents, blocks)
+        ])
         if state is not None:
             fading = jnp.exp2((state[0] - top) * to_exponent)
             total = state[1] * fading + total
@@ -220,20 +236,18 @@
     for batch in range(batches):
         for array, kind in ((k_all, 1), (v_all, 2)):
             gathered(array, kind, batch)
-        if batch:
-            state = absorb(state, 1, batch - 1)
-        state = absorb(state, 0, batch)
-    state = absorb(state, 1, batches - 1)
+        state = absorb(state, ([(1, batch - 1)] if batch else []) + [(0, batch)])
+    state = absorb(state, [(1, batches - 1)])
 
     out_send[...] = (state[2] / state[1]).astype(jnp.bfloat16).reshape(heads, tokens, HEAD_DIM)
     for index in far_first:
-        remote(out_send.at[index], out_hbm.at[:, columns(mine)], o_send, o_recv, peer(home(index)))
+        remote(out_send.at[index], out_hbm.at[:, columns(mine)], o_send, o_recv, home_peers[index])
     pltpu.make_async_copy(out_send.at[0], out_hbm.at[:, columns(mine)], o_recv).start()
 
     for kind in range(3):
         wait_bytes(q_land.at[pl.ds(0, heads - 1)], a_send.at[kind])
     for array, kind in ((k_all, 0), (v_all, 1)):
-        wait_bytes(array.at[0, pl.ds(0, RING - 1)], y_send.at[kind])
+        wait_bytes(array.at[0, :, pl.ds(0, RING - 1)], y_send.at[kind])
         wait_bytes(array.at[1], s_send.at[kind])
     wait_bytes(q_land.at[pl.ds(0, heads - 1)], o_send)
     wait_bytes(out_hbm, o_recv)
@@ -253,6 +267,7 @@
         scratch_shapes=[
             pltpu.VMEM((tokens, features), bf16),
             pltpu.VMEM((tokens, features), bf16),
+            pltpu.VMEM((tokens, features), bf16),
             pltpu.VMEM((heads, HEAD_DIM), jnp.float32),
             pltpu.VMEM((heads, HEAD_DIM), jnp.float32),
             pltpu.VMEM((2, tokens, HEAD_DIM), jnp.float32),
@@ -262,7 +277,7 @@
             pltpu.VMEM((CORES, batches, RING, BATCH, tokens, HEAD_DIM), bf16),
             pltpu.VMEM((CORES, batches, RING, BATCH, tokens, HEAD_DIM), bf16),
             pltpu.VMEM((heads, tokens, HEAD_DIM), bf16),
-            pltpu.SemaphoreType.DMA((4,)),
+            pltpu.SemaphoreType.DMA((5,)),
             pltpu.SemaphoreType.DMA((2,)),
             pltpu.SemaphoreType.DMA((3,)),
             pltpu.SemaphoreType.DMA((3, heads // PIECE)),

time: 33.9 us -> 33.6 us (level)
  Pallas kernels: 33.2 us -> 32.8 us
    pallas_call x1, Pallas kernels: 33.2 us -> 32.8 us  [on_device(): pl.pallas_call(kernel, out_shape=jax.ShapeDtypeStruct((tokens, features),...]
where the time goes in v4:
time: 33.6 us; the launch traced here: 33.5 us
  Pallas kernels  32.8 us (98%)
  local copies, waits for them, and re-layouts  0.64 us (2%)
    pallas_call x1, Pallas kernels, on_device(): pl.pallas_call(kernel, out_shape=jax.ShapeDtypeStruct((tokens, features),...  32.8 us

profile of v4, /device:TPU:1, one launch (start us, length us, event | category | flops | bytes accessed | tf_op | source)
XLA Modules:
  0.0 33.5 jit_solution(6523403560086278016)
XLA Ops:
  0.0 32.8 %shard_map.55 = bf16[24,2048]{1,0:T(8,128)(2,1)S(1)} custom-call(bf16[24,2048]{1,0:T(8,128)(2,1)} %q_hbm.1, bf16[24,2048]{1,0:T(8,128)(2,1)} %k_hbm.1, bf16[24,2048]{1,0:T(8,128)(2,1)} %v_hbm.1, f32[16,128]{1,0:T(8,128)} %bitcast.2, f32[16,128]{1,0:T(8,128)} %bitcast.3), custom_call_target="tpu_custom_call" | custom-call | tf_op jit(solution)/shard_map/pallas_call | solution.py:262
  32.8 0.6 %copy.7 = bf16[24,2048]{1,0:T(8,128)(2,1)} copy(bf16[24,2048]{1,0:T(8,128)(2,1)S(1)} %shard_map.55) | data formatting | bytes 196608

commit v5 on v4

--- a/solution.py
+++ b/solution.py
@@ -202,9 +202,9 @@
     query = q_land[...].reshape(keys, HEAD_DIM)
     to_exponent = math.log2(math.e) * HEAD_DIM ** (-0.5)
 
-    def absorb(state, blocks):
+    def absorb(state, query, blocks, ready=False):
         for half, batch in blocks:
-            if half:
+            if half and not ready:
                 wait_bytes(v_all.at[1, batch], s_recv.at[1, batch])
                 wait_bytes(k_all.at[1, batch], s_recv.at[0, batch])
         scores = [
@@ -236,12 +236,16 @@
     for batch in range(batches):
         for array, kind in ((k_all, 1), (v_all, 2)):
             gathered(array, kind, batch)
-        state = absorb(state, ([(1, batch - 1)] if batch else []) + [(0, batch)])
-    state = absorb(state, [(1, batches - 1)])
-
-    out_send[...] = (state[2] / state[1]).astype(jnp.bfloat16).reshape(heads, tokens, HEAD_DIM)
-    for index in far_first:
-        remote(out_send.at[index], out_hbm.at[:, columns(mine)], o_send, o_recv, home_peers[index])
+        state = absorb(state, query, ([(1, batch - 1)] if batch else []) + [(0, batch)])
+    middle = heads // 2
+    for first in (middle, 0):
+        rows = slice(first * tokens, (first + middle) * tokens)
+        _, total, mixed = absorb(
+            tuple(part[rows] for part in state), query[rows], [(1, batches - 1)], ready=first == 0
+        )
+        out_send[first:first + middle] = (mixed / total).astype(jnp.bfloat16).reshape(middle, tokens, HEAD_DIM)
+        for index in range(first + middle - 1, max(first, 1) - 1, -1):
+            remote(out_send.at[index], out_hbm.at[:, columns(mine)], o_send, o_recv, home_peers[index])
     pltpu.make_async_copy(out_send.at[0], out_hbm.at[:, columns(mine)], o_recv).start()
 
     for kind in range(3):

time: 33.6 us -> 33.5 us (level)
  no operation moved by 1% of the time
where the time goes in v5:
time: 33.5 us; the launch traced here: 33.4 us
  Pallas kernels  32.7 us (98%)
  local copies, waits for them, and re-layouts  0.64 us (2%)
    pallas_call x1, Pallas kernels, on_device(): pl.pallas_call(kernel, out_shape=jax.ShapeDtypeStruct((tokens, features),...  32.7 us

profile of v5, /device:TPU:1, one launch (start us, length us, event | category | flops | bytes accessed | tf_op | source)
XLA Modules:
  0.0 33.4 jit_solution(10008660382216215833)
XLA Ops:
  0.0 32.7 %shard_map.55 = bf16[24,2048]{1,0:T(8,128)(2,1)S(1)} custom-call(bf16[24,2048]{1,0:T(8,128)(2,1)} %q_hbm.1, bf16[24,2048]{1,0:T(8,128)(2,1)} %k_hbm.1, bf16[24,2048]{1,0:T(8,128)(2,1)} %v_hbm.1, f32[16,128]{1,0:T(8,128)} %bitcast.2, f32[16,128]{1,0:T(8,128)} %bitcast.3), custom_call_target="tpu_custom_call" | custom-call | tf_op jit(solution)/shard_map/pallas_call | solution.py:266
  32.7 0.6 %copy.7 = bf16[24,2048]{1,0:T(8,128)(2,1)} copy(bf16[24,2048]{1,0:T(8,128)(2,1)S(1)} %shard_map.55) | data formatting | bytes 196608

commit v6 on v5

--- a/solution.py
+++ b/solution.py
@@ -133,13 +133,14 @@
     def wait_bytes(ref, sem):
         pltpu.make_async_copy(ref, ref, sem).wait()
 
-    def exchange(pick, slot, kind):
-        for index in far_first:
+    def exchange(pick, slot, kind, chosen=far_first):
+        for index in chosen:
             remote(
                 pick(servers[index]), slot(index), a_send.at[kind], a_recv.at[kind, index // PIECE],
                 server_peers[index],
             )
-        pltpu.make_async_copy(pick(mine), slot(0), a_recv.at[kind, 0]).start()
+        if 1 in chosen:
+            pltpu.make_async_copy(pick(mine), slot(0), a_recv.at[kind, 0]).start()
 
     exchange(lambda to: v_in.at[:, columns(to)], lambda i: v_all.at[0, i // BATCH, 0, i % BATCH], 2)
 
@@ -151,16 +152,21 @@
     sum_copy.wait()
     scale = lax.rsqrt((sums[0] + sums[1]) / (HEADS * HEAD_DIM) + 1e-06)
 
-    def prepare(source, factor, gain, target):
-        for head in range(heads):
-            rows = source[:, head * HEAD_DIM:(head + 1) * HEAD_DIM].astype(jnp.float32)
-            rows = rows * factor * gain[head:head + 1, :]
+    def prepare(source, factor, gain, target, chosen):
+        for index in chosen:
+            head = servers[index]
+            rows = source[:, columns(head)].astype(jnp.float32)
+            rows = rows * factor * gain[pl.ds(head, 1), :]
             rows = rows * cosine + pltpu.roll(rows, HEAD_DIM // 2, 1) * sine
             target[head] = rows.astype(jnp.bfloat16)
 
-    prepare(k_in, scale[:, HEAD_DIM // 2:HEAD_DIM // 2 + 1], k_gain, k_send)
-    exchange(lambda to: k_send.at[to], lambda i: k_all.at[0, i // BATCH, 0, i % BATCH], 1)
-    prepare(q_in, scale[:, 0:1], q_gain, q_send)
+    half = heads // 2
+    key_scale = scale[:, HEAD_DIM // 2:HEAD_DIM // 2 + 1]
+    for chosen in (range(heads - 1, half - 1, -1), range(half - 1, -1, -1)):
+        prepare(k_in, key_scale, k_gain, k_send, chosen)
+        sent = [index for index in chosen if index]
+        exchange(lambda to: k_send.at[to], lambda i: k_all.at[0, i // BATCH, 0, i % BATCH], 1, sent)
+    prepare(q_in, scale[:, 0:1], q_gain, q_send, range(heads))
     exchange(lambda to: q_send.at[to], lambda i: q_land.at[i], 0)
 
     batches = heads // BATCH

time: 33.5 us -> 33.5 us (level)
  no operation moved by 1% of the time
where the time goes in v6:
time: 33.5 us; the launch traced here: 33.4 us
  Pallas kernels  32.7 us (98%)
  local copies, waits for them, and re-layouts  0.64 us (2%)
    pallas_call x1, Pallas kernels, on_device(): pl.pallas_call(kernel, out_shape=jax.ShapeDtypeStruct((tokens, features),...  32.7 us

profile of v6, /device:TPU:1, one launch (start us, length us, event | category | flops | bytes accessed | tf_op | source)
XLA Modules:
  0.0 33.4 jit_solution(12420482288110790651)
XLA Ops:
  0.0 32.7 %shard_map.55 = bf16[24,2048]{1,0:T(8,128)(2,1)S(1)} custom-call(bf16[24,2048]{1,0:T(8,128)(2,1)} %q_hbm.1, bf16[24,2048]{1,0:T(8,128)(2,1)} %k_hbm.1, bf16[24,2048]{1,0:T(8,128)(2,1)} %v_hbm.1, f32[16,128]{1,0:T(8,128)} %bitcast.2, f32[16,128]{1,0:T(8,128)} %bitcast.3), custom_call_target="tpu_custom_call" | custom-call | tf_op jit(solution)/shard_map/pallas_call | solution.py:272
  32.7 0.6 %copy.7 = bf16[24,2048]{1,0:T(8,128)(2,1)} copy(bf16[24,2048]{1,0:T(8,128)(2,1)S(1)} %shard_map.55) | data formatting | bytes 196608
